TPU v7x, 32 devices: a whole 2x2x4 slice. The times are simulated.
32 devices in a mesh: noise: 4 (over z), dp: 8 (over y, x, core).
Axes of the slice: x: 2, y: 2, z: 4, core: 2. Of those that a mesh axis runs over, the one named last changes fastest.
Arguments:
- noise_points: float32 [6144, 512], P('noise'), may hold values from -1.5 to 1.5
- data_points: float32 [3072, 512], P('dp', 'noise'), may hold values from -1.5 to 1.5
- noise_blocks: int32 [4], P('noise'), may hold values from 1 to 12, as said below
- data_blocks: int32 [8], P('dp'), may hold values from 1 to 3, as said below
Outputs:
- noise_potential: float32 [6144], P('noise')
- data_potential: float32 [3072], P('dp')
- noise_target: float32 [512, 6144], P('dp', 'noise')
- data_target: float32 [512, 3072], P('noise', 'dp')
Inputs may be any that keep to these rules, and one draw needn't show every extreme that they name: `noise_blocks`: blocks 0 up to this count of each device's 12 slots are live, the rest padding; some device has all 12 live. `data_blocks`: blocks 0 up to this count of each device's 3 slots are live, the rest padding; some device has all 3 live.
All inputs are finite; a program needn't handle non-finite values.
Results may differ from a plain program's by a relative error of at most 0.0003.
Values sent between devices are 32-bit elements; how exact they have to be, the bound alone decides.
A program may use at most 64 MiB of HBM per device.

v0:
```python
import jax
import jax.numpy as jnp
from jax import lax
from jax.sharding import PartitionSpec as P

BLOCK = 128
ITERS = 3


SMOOTHING_TEMP = 0.125


def combined_all(shard, axis, combine):
    everything = jax.tree.map(lambda part: lax.all_gather(part, axis), shard)
    initial = jax.tree.map(lambda part: part[0], everything)

    def lap(k, so_far):
        return combine(so_far, jax.tree.map(lambda part: part[k], everything))

    return lax.fori_loop(1, lax.axis_size(axis), lap, initial)


def pair_cost(rows, cols, col_sq):
    row_sq = jnp.sum(rows * rows, axis=1)
    cross = jnp.dot(
        rows, cols.T, precision=lax.Precision.HIGHEST, preferred_element_type=jnp.float32
    )
    return row_sq[:, None] + col_sq[None, :] - 2.0 * cross


def combine_peaks(first, second):
    top = jnp.maximum(first[0], second[0])
    return (top, first[1] * jnp.exp(first[0] - top) + second[1] * jnp.exp(second[0] - top))


def row_threshold(pair_scores):
    local = jnp.max(pair_scores, axis=1)
    mass = jnp.sum(jnp.exp(pair_scores - local[:, None]), axis=1)
    top, mass = combined_all((local, mass), "dp", combine_peaks)
    return top + jnp.log(mass)


def column_level(pair_scores):
    local = jnp.max(pair_scores, axis=0)
    mass = jnp.sum(jnp.exp(pair_scores - local[None, :]), axis=0)
    top, mass = combined_all((local, mass), "noise", combine_peaks)
    return top + jnp.log(mass)


def on_device(noise_points, data_points, noise_blocks, data_blocks):
    rows_dev = noise_points.shape[0]
    cols_dev = data_points.shape[0]
    noise_total = lax.psum((noise_blocks * BLOCK).astype(jnp.float32), "noise")
    data_total = lax.psum((data_blocks * BLOCK).astype(jnp.float32), "dp")
    log_noise_mass = -jnp.log(noise_total[0])
    log_data_mass = -jnp.log(data_total[0])
    data_full = lax.all_gather(data_points, "noise", axis=1, tiled=True)
    row_active = jnp.arange(rows_dev, dtype=jnp.int32) < noise_blocks[0] * BLOCK
    column_active = jnp.arange(cols_dev, dtype=jnp.int32) < data_blocks[0] * BLOCK
    col_sq = jnp.sum(data_full * data_full, axis=1)
    transport_cost = pair_cost(noise_points, data_full, col_sq)
    data_potential = jnp.zeros((cols_dev,), jnp.float32)
    noise_potential = jnp.zeros((rows_dev,), jnp.float32)
    for turn in range(ITERS):
        pair_scores = jnp.where(
            column_active[None, :],
            (data_potential[None, :] - transport_cost) / SMOOTHING_TEMP + log_data_mass,
            -jnp.inf,
        )
        noise_potential = jnp.where(row_active, -SMOOTHING_TEMP * row_threshold(pair_scores), 0.0)
        pair_scores = jnp.where(
            row_active[:, None],
            (noise_potential[:, None] - transport_cost) / SMOOTHING_TEMP + log_noise_mass,
            -jnp.inf,
        )
        data_potential = jnp.where(column_active, -SMOOTHING_TEMP * column_level(pair_scores), 0.0)
    pair_scores = jnp.where(
        column_active[None, :],
        (data_potential[None, :] - transport_cost) / SMOOTHING_TEMP + log_data_mass,
        -jnp.inf,
    )
    level = row_threshold(pair_scores)
    both_live = row_active[:, None] & column_active[None, :]
    noise_weights = jnp.where(both_live, jnp.exp(pair_scores - level[:, None]), 0.0)
    data_weights = jnp.where(
        both_live,
        jnp.exp(
            (noise_potential[:, None] + data_potential[None, :] - transport_cost) / SMOOTHING_TEMP
            + log_noise_mass
        ),
        0.0,
    )
    coords = data_full
    noise_target = lax.psum_scatter(
        lax.dot_general(
            coords,
            noise_weights,
            (((0,), (1,)), ((), ())),
            precision=lax.Precision.HIGHEST,
            preferred_element_type=jnp.float32,
        ),
        "dp",
        scatter_dimension=0,
        tiled=True,
    )
    coords = noise_points
    data_target = lax.psum_scatter(
        lax.dot_general(
            coords,
            data_weights,
            (((0,), (0,)), ((), ())),
            precision=lax.Precision.HIGHEST,
            preferred_element_type=jnp.float32,
        ),
        "noise",
        scatter_dimension=0,
        tiled=True,
    )
    return (noise_potential, data_potential, noise_target, data_target)


def solution(mesh):
    return jax.shard_map(
        on_device,
        mesh=mesh,
        in_specs=(P("noise", None), P("dp", "noise"), P("noise"), P("dp")),
        out_specs=(P("noise"), P("dp"), P("dp", "noise"), P("noise", "dp")),
        check_vma=False,
    )
```

profile of v0, /device:TPU:0, one launch (start us, length us, event | category | flops | bytes accessed | tf_op | source)
XLA Modules:
  0.0 283.6 jit_solution(7583929042006059796)
XLA Ops:
  7.2 0.0 reduce-scatter.5.cloned.1.call-start
  7.9 15.6 %psum.14 = f32[1]{0:T(128)} all-reduce(f32[1]{0:T(128)S(6)} %convert_element_type.6), channel_id=1, replica_groups=mesh['noise'=4,'dp'=8] {'dp'}, use_global_device_ids=true, to_apply=%region_2.0 | all-reduce | flops 1 | bytes 8 | tf_op jit(solution)/shard_map/psum | solution.py:54
  24.2 19.1 %all_gather.87 = f32[384,512]{1,0:T(8,128)S(1)} all-gather(f32[384,128]{1,0:T(8,128)} %param.19), channel_id=1, replica_groups=mesh['noise'=4,'dp'=8] {'noise'}, dimensions={1}, use_global_device_ids=true | all-gather | bytes 983040 | tf_op jit(solution)/shard_map/all_gather | solution.py:57
  43.3 0.1 multiply_reduce_fusion.1
  43.5 2.2 multiply_reduce_fusion
  45.7 4.3 %fusion.9 = (f32[1536]{0:T(1024)S(1)}, f32[1536,384]{0,1:T(8,128)S(1)}) fusion(f32[]{:T(128)} %bitcast.2, pred[384]{0:T(512)(128)(4,1)S(1)} %iota_compare_fusion.1, f32[1536,512]{1,0:T(8,128)S(1)} %copy-done, f32[384,512]{1,0:T(8,128)S(1)} %all_gather.87, f32[384]{0:T(512)S(1)} %multiply_reduce_fusion.1, f32[1536]{0:T(1024)S(1)} %multiply_reduce_fusion), kind=kOutput, calls=%fused_computation.49 | convolution fusion | flops 3628595712 | bytes 6305668 | tf_op jit(solution)/shard_map/dot_general | solution.py:25
  50.0 0.7 exponential_reduce_fusion.6
  50.6 9.3 %all-gather.15 = f32[8,1,1536]{2,1,0:T(1,128)S(1)} all-gather(f32[1,1,1536]{2,1,0:T(1,128)S(1)} %reshape.84), channel_id=3, replica_groups=mesh['noise'=4,'dp'=8] {'dp'}, dimensions={0}, use_global_device_ids=true | all-gather | bytes 55296 | tf_op jit(solution)/shard_map/all_gather | solution.py:14
  60.0 8.0 %all-gather.14 = f32[8,1,1536]{2,1,0:T(1,128)S(1)} all-gather(f32[1,1,1536]{2,1,0:T(1,128)S(1)} %reshape.82), channel_id=2, replica_groups=mesh['noise'=4,'dp'=8] {'dp'}, dimensions={0}, use_global_device_ids=true | all-gather | bytes 55296 | tf_op jit(solution)/shard_map/all_gather | solution.py:14
  68.0 0.6 while.119
  69.3 10.7 %psum.15 = f32[1]{0:T(128)} all-reduce(f32[1]{0:T(128)S(6)} %convert_element_type.7), channel_id=1, replica_groups=mesh['noise'=4,'dp'=8] {'noise'}, use_global_device_ids=true, to_apply=%region_7.8 | all-reduce | flops 1 | bytes 8 | tf_op jit(solution)/shard_map/psum | solution.py:53
  80.8 0.5 fusion.10
  81.2 0.7 exponential_reduce_fusion.5
  81.9 11.9 %all-gather.17 = f32[4,1,384]{2,1,0:T(1,128)S(1)} all-gather(f32[1,1,384]{2,1,0:T(1,128)S(1)} %reshape.88), channel_id=5, replica_groups=mesh['noise'=4,'dp'=8] {'noise'}, dimensions={0}, use_global_device_ids=true | all-gather | bytes 7680 | tf_op jit(solution)/shard_map/all_gather | solution.py:14
  93.8 11.9 %all-gather.16 = f32[4,1,384]{2,1,0:T(1,128)S(1)} all-gather(f32[1,1,384]{2,1,0:T(1,128)S(1)} %reshape.86), channel_id=4, replica_groups=mesh['noise'=4,'dp'=8] {'noise'}, dimensions={0}, use_global_device_ids=true | all-gather | bytes 7680 | tf_op jit(solution)/shard_map/all_gather | solution.py:14
  105.7 0.2 while.120
  105.9 0.5 fusion.11
  106.4 0.7 exponential_reduce_fusion.4
  107.1 9.1 %all-gather.19 = f32[8,1,1536]{2,1,0:T(1,128)S(1)} all-gather(f32[1,1,1536]{2,1,0:T(1,128)S(1)} %reshape.92), channel_id=7, replica_groups=mesh['noise'=4,'dp'=8] {'dp'}, dimensions={0}, use_global_device_ids=true | all-gather | bytes 55296 | tf_op jit(solution)/shard_map/all_gather | solution.py:14
  116.3 8.4 %all-gather.18 = f32[8,1,1536]{2,1,0:T(1,128)S(1)} all-gather(f32[1,1,1536]{2,1,0:T(1,128)S(1)} %reshape.90), channel_id=6, replica_groups=mesh['noise'=4,'dp'=8] {'dp'}, dimensions={0}, use_global_device_ids=true | all-gather | bytes 55296 | tf_op jit(solution)/shard_map/all_gather | solution.py:14
  124.7 0.6 while.121
  125.4 0.5 fusion.12
  125.8 0.7 exponential_reduce_fusion.3
  126.5 11.9 %all-gather.21 = f32[4,1,384]{2,1,0:T(1,128)S(1)} all-gather(f32[1,1,384]{2,1,0:T(1,128)S(1)} %reshape.96), channel_id=9, replica_groups=mesh['noise'=4,'dp'=8] {'noise'}, dimensions={0}, use_global_device_ids=true | all-gather | bytes 7680 | tf_op jit(solution)/shard_map/all_gather | solution.py:14
  138.4 11.9 %all-gather.20 = f32[4,1,384]{2,1,0:T(1,128)S(1)} all-gather(f32[1,1,384]{2,1,0:T(1,128)S(1)} %reshape.94), channel_id=8, replica_groups=mesh['noise'=4,'dp'=8] {'noise'}, dimensions={0}, use_global_device_ids=true | all-gather | bytes 7680 | tf_op jit(solution)/shard_map/all_gather | solution.py:14
  150.3 0.2 while.122
  150.5 0.5 fusion.13
  151.0 0.7 exponential_reduce_fusion.2
  151.7 9.1 %all-gather.23 = f32[8,1,1536]{2,1,0:T(1,128)S(1)} all-gather(f32[1,1,1536]{2,1,0:T(1,128)S(1)} %reshape.100), channel_id=11, replica_groups=mesh['noise'=4,'dp'=8] {'dp'}, dimensions={0}, use_global_device_ids=true | all-gather | bytes 55296 | tf_op jit(solution)/shard_map/all_gather | solution.py:14
  160.9 8.2 %all-gather.22 = f32[8,1,1536]{2,1,0:T(1,128)S(1)} all-gather(f32[1,1,1536]{2,1,0:T(1,128)S(1)} %reshape.98), channel_id=10, replica_groups=mesh['noise'=4,'dp'=8] {'dp'}, dimensions={0}, use_global_device_ids=true | all-gather | bytes 55296 | tf_op jit(solution)/shard_map/all_gather | solution.py:14
  169.1 0.6 while.123
  169.8 0.5 fusion.14
  170.2 0.7 exponential_reduce_fusion.1
  170.9 11.9 %all-gather.25 = f32[4,1,384]{2,1,0:T(1,128)S(1)} all-gather(f32[1,1,384]{2,1,0:T(1,128)S(1)} %reshape.104), channel_id=13, replica_groups=mesh['noise'=4,'dp'=8] {'noise'}, dimensions={0}, use_global_device_ids=true | all-gather | bytes 7680 | tf_op jit(solution)/shard_map/all_gather | solution.py:14
  182.8 11.9 %all-gather.24 = f32[4,1,384]{2,1,0:T(1,128)S(1)} all-gather(f32[1,1,384]{2,1,0:T(1,128)S(1)} %reshape.102), channel_id=12, replica_groups=mesh['noise'=4,'dp'=8] {'noise'}, dimensions={0}, use_global_device_ids=true | all-gather | bytes 7680 | tf_op jit(solution)/shard_map/all_gather | solution.py:14
  194.7 0.2 while.124
  195.0 7.4 %fusion.15 = f32[512,384]{0,1:T(8,128)} fusion(f32[1536,512]{1,0:T(8,128)} %param.18, f32[1536,384]{0,1:T(8,128)S(1)} %get-tuple-element.1056, f32[384]{0:T(512)S(1)} %multiply_select_fusion.3, f32[1536]{0:T(1024)S(1)} %multiply_select_fusion, f32[]{:T(128)} %bitcast.3, pred[1536]{0:T(1024)(128)(4,1)S(1)} %iota_compare_fusion, ...), kind=kOutput, calls=%fused_computation.55 | convolution fusion | flops 3627417600 | bytes 6301060 | tf_op jit(solution)/shard_map/dot_general | solution.py:108
  202.4 0.0 reduce-scatter.7.cloned.1.call-start
  202.4 0.5 fusion.16
  202.9 0.7 exponential_reduce_fusion
  203.6 9.1 %all-gather.27 = f32[8,1,1536]{2,1,0:T(1,128)S(1)} all-gather(f32[1,1,1536]{2,1,0:T(1,128)S(1)} %reshape.108), channel_id=15, replica_groups=mesh['noise'=4,'dp'=8] {'dp'}, dimensions={0}, use_global_device_ids=true | all-gather | bytes 55296 | tf_op jit(solution)/shard_map/all_gather | solution.py:14
  212.8 8.4 %all-gather.26 = f32[8,1,1536]{2,1,0:T(1,128)S(1)} all-gather(f32[1,1,1536]{2,1,0:T(1,128)S(1)} %reshape.106), channel_id=14, replica_groups=mesh['noise'=4,'dp'=8] {'dp'}, dimensions={0}, use_global_device_ids=true | all-gather | bytes 55296 | tf_op jit(solution)/shard_map/all_gather | solution.py:14
  221.2 0.6 while.125
  221.9 7.5 %convolution_bitcast_fusion = f32[512,1536]{0,1:T(8,128)} fusion(f32[384,512]{1,0:T(8,128)S(1)} %all_gather.87, f32[1536,384]{0,1:T(8,128)S(1)} %get-tuple-element.1056, f32[1536]{0:T(1024)S(1)} %log_add_fusion, f32[384]{0:T(512)S(1)} %multiply_select_fusion.3, f32[]{:T(128)} %bitcast.2, pred[1536]{0:T(1024)(128)(4,1)S(1)} %iota_compare_fusion, ...), kind=kOutput, calls=%fused_computation.21 | convolution fusion | flops 3628007424 | bytes 6301060 | tf_op jit(solution)/shard_map/dot_general | solution.py:95
  229.3 3.5 %copy.12 = f32[512,1536]{1,0:T(8,128)} copy(f32[512,1536]{0,1:T(8,128)} %convolution_bitcast_fusion) | data formatting | bytes 6291456
  232.9 0.0 reduce-scatter.5.cloned.1.call-done
  232.9 1.7 copy.11
  234.7 42.1 %reduce-scatter.7.cloned.1.call-done = f32[64,1536]{1,0:T(8,128)} async-done(((f32[512,1536]{1,0:T(8,128)}), f32[64,1536]{1,0:T(8,128)}) %reduce-scatter.7.cloned.1.call-update) | async-done | bytes 393232
  (133 shorter events, 2.5 us)
Async XLA Ops:
  7.2 225.8 %reduce-scatter.5.cloned.1.call-start = ((), (), s32[]{:S(2)}) async-start(), calls=%async_computation.2 | async-start | bytes 983040 | tf_op jit(solution)/shard_map/reduce_scatter | solution.py:107
  24.2 21.5 %copy-start = (f32[1536,512]{1,0:T(8,128)S(1)}, f32[1536,512]{1,0:T(8,128)}, u32[]{:S(2)}) copy-start(f32[1536,512]{1,0:T(8,128)} %param.18) | copy-start | bytes 9437188
  169.7 25.2 %copy-start.1 = (f32[1536]{0:T(1024)}, f32[1536]{0:T(1024)S(1)}, u32[]{:S(2)}) copy-start(f32[1536]{0:T(1024)S(1)} %multiply_select_fusion) | copy-start | bytes 18436
  194.9 26.9 %copy-start.2 = (f32[384]{0:T(512)}, f32[384]{0:T(512)S(1)}, u32[]{:S(2)}) copy-start(f32[384]{0:T(512)S(1)} %multiply_select_fusion.3) | copy-start | bytes 4612
  202.4 74.4 %reduce-scatter.7.cloned.1.call-start = ((), (), s32[]{:S(2)}) async-start(), calls=%async_computation.3 | async-start | bytes 3538944
Sparse Core Ops, SparseCore 0:
  202.5 20.7 reduce-scatter.4
  233.0 43.7 reduce-scatter.6
where the time goes:
time: 284 us
  blocking collectives  186 us (65%)
  waiting for transfers between devices  42.2 us (15%)
  matrix products  19.1 us (7%)
  between operations  17.1 us (6%)
  other arithmetic  10.7 us (4%)
  local copies, waits for them, and re-layouts  7.06 us (2%)
    all_gather x14, blocking collectives, combined_all(): everything = jax.tree.map(lambda part: lax.all_gather(part, axis), shard)  141 us
    unnamed x3, waiting for transfers between devices  42.2 us
    all_gather x1, blocking collectives, on_device(): data_full = lax.all_gather(data_points, 'noise', axis=1, tiled=True)  19.1 us
    psum x1, blocking collectives, on_device(): data_total = lax.psum((data_blocks * BLOCK).astype(jnp.float32), 'dp')  15.6 us
    psum x1, blocking collectives, on_device(): noise_total = lax.psum((noise_blocks * BLOCK).astype(jnp.float32), 'noise')  10.7 us
    dot_general x1, matrix products, on_device(): lax.dot_general(coords, noise_weights, (((0,), (1,)), ((), ())), precisio...  7.45 us
    dot_general x1, matrix products, on_device(): lax.dot_general(coords, data_weights, (((0,), (0,)), ((), ())), precision...  7.39 us
  transfers between devices with their start and end apart: 2, of which 1 were waited for; matrix products, arithmetic and copies ran while one was open for 5% of the time, Pallas kernels for 0%

commit v1 on v0

v1 whole, which is shorter than its diff:
```python
import functools

import jax
import jax.numpy as jnp
from jax import lax
from jax.experimental import pallas as pl
from jax.experimental.pallas import tpu as pltpu
from jax.sharding import PartitionSpec as P

BLOCK = 128
ITERS = 3
SMOOTHING_TEMP = 0.125
TILE = 256
MESH = pl.DeviceIdType.MESH
F32 = jnp.float32
BF16 = jnp.bfloat16
NT = (((1,), (1,)), ((), ()))


def split(x):
    hi = x.astype(BF16)
    return hi, (x - hi.astype(F32)).astype(BF16)


def dot3(ahi, alo, bhi, blo):
    d = functools.partial(jnp.dot, preferred_element_type=F32)
    return d(ahi, bhi) + (d(ahi, blo) + d(alo, bhi))


def kernel(n, nz, x_ref, y_ref, nb_ref, db_ref, f_ref, g_ref, nt_ref, dt_ref,
           dbuf, dfull, yt, kt, gmb, fmrow, facrow, xsq, xhi, xlo, whi, wlo, dhi, dlo,
           rst, cst, acc, rb, ptmp, pbuf, zbuf,
           ag_s, ag_r, rs_s, rs_r, cs_s, cs_r, h_s, h_r, z_s, z_r):
    me = lax.axis_index("dp")
    mz = lax.axis_index("noise")
    rows, coords = x_ref.shape
    cols, cz = y_ref.shape
    nr, nc = rows // BLOCK, cols // BLOCK
    cb = coords // n
    steps = n.bit_length() - 1

    barrier = pltpu.get_barrier_semaphore()
    for o in range(1, n):
        pl.semaphore_signal(barrier, inc=1, device_id={"dp": lax.rem(me + o, n)}, device_id_type=MESH)
    for o in range(1, nz):
        pl.semaphore_signal(barrier, inc=1, device_id={"noise": lax.rem(mz + o, nz)}, device_id_type=MESH)
    pl.semaphore_wait(barrier, n + nz - 2)

    def copy(src, dst, ssem, rsem, axis, to):
        return pltpu.make_async_remote_copy(
            src_ref=src, dst_ref=dst, send_sem=ssem, recv_sem=rsem,
            device_id={axis: to}, device_id_type=MESH)

    def spread(buf, ssem, rsem, axis, size, mine):
        sent = []
        for o in range(1, size):
            c = copy(buf.at[mine], buf.at[mine], ssem.at[o], rsem.at[mine], axis, lax.rem(mine + o, size))
            c.start()
            sent.append(c)
        return sent

    def arrive(buf, ssem, rsem, axis, size, mine):
        for o in range(1, size):
            src = lax.rem(mine + size - o, size)
            copy(buf.at[src], buf.at[src], ssem.at[o], rsem.at[src], axis, src).wait_recv()

    pending = []
    dbuf[mz] = y_ref[...]
    pending += spread(dbuf, ag_s, ag_r, "noise", nz, mz)

    ones = jnp.ones((8, coords), F32)

    def prep(t, _):
        at = pl.ds(pl.multiple_of(t * TILE, TILE), TILE)
        x = x_ref[at, :]
        hi, lo = split(x)
        xhi[at, :] = hi
        xlo[at, :] = lo
        xsq[:, at] = lax.dot_general(ones, x * x, NT, precision=lax.Precision.HIGHEST,
                                     preferred_element_type=F32)[0:1, :]
        return 0

    lax.fori_loop(0, rows // TILE, prep, 0)

    live_i = lax.broadcasted_iota(jnp.int32, (nr, BLOCK), 0) < nb_ref[0]
    live_j = lax.broadcasted_iota(jnp.int32, (nc, BLOCK), 0) < db_ref[0]
    eye = (lax.broadcasted_iota(jnp.int32, (BLOCK, BLOCK), 0)
           == lax.broadcasted_iota(jnp.int32, (BLOCK, BLOCK), 1))

    def set_gm(g):
        gm = jnp.where(live_j, g, -jnp.inf)
        for k in range(nc):
            gmb[k * BLOCK:(k + 1) * BLOCK, :] = jnp.broadcast_to(gm[k:k + 1, :], (BLOCK, BLOCK)).T

    set_gm(jnp.zeros((nc, BLOCK), F32))

    arrive(dbuf, ag_s, ag_r, "noise", nz, mz)
    for k in range(nz):
        dfull[:, k * cz:(k + 1) * cz] = dbuf[k]
    ysq = jnp.sum(dfull[...] * dfull[...], axis=1, keepdims=True)

    def cost(t, _):
        at = pl.ds(pl.multiple_of(t * TILE, TILE), TILE)
        cross = lax.dot_general(dfull[...], x_ref[at, :], NT, precision=lax.Precision.HIGHEST,
                                preferred_element_type=F32)
        kt[:, at] = (2.0 * cross - (xsq[:, at] + ysq)) * (1.0 / SMOOTHING_TEMP)
        return 0

    lax.fori_loop(0, rows // TILE, cost, 0)

    def row_pass(r, keep):
        def body(c, _):
            at = pl.ds(pl.multiple_of(c * BLOCK, BLOCK), BLOCK)
            s = kt[:, at] + gmb[...]
            top = jnp.max(s, axis=0, keepdims=True)
            e = jnp.exp(s - top)
            rst[r, me, pl.ds(c, 1), :] = top
            rst[r, me, pl.ds(nr + c, 1), :] = jnp.sum(e, axis=0, keepdims=True)
            if keep:
                hi, lo = split(e)
                whi[:, at] = hi
                wlo[:, at] = lo
            return 0

        lax.fori_loop(0, nr, body, 0)
        rst[r, me, 2 * nr:2 * nr + 8, :] = jnp.full((8, BLOCK), db_ref[0].astype(F32), F32)
        return spread(rst.at[r], rs_s.at[r], rs_r.at[r], "dp", n, me)

    def col_pass(r):
        def body(k, _):
            s = kt[pl.ds(pl.multiple_of(k * BLOCK, BLOCK), BLOCK), :] + fmrow[...]
            top = jnp.max(s, axis=1, keepdims=True)
            mass = jnp.sum(jnp.exp(s - top), axis=1, keepdims=True)
            cst[r, mz, pl.ds(k, 1), :] = jnp.sum(jnp.where(eye, top, 0.0), axis=0, keepdims=True)
            cst[r, mz, pl.ds(nc + k, 1), :] = jnp.sum(jnp.where(eye, mass, 0.0), axis=0, keepdims=True)
            return 0

        lax.fori_loop(0, nc, body, 0)
        cst[r, mz, 2 * nc:2 * nc + 1, :] = jnp.full((1, BLOCK), nb_ref[0].astype(F32), F32)
        return spread(cst.at[r], cs_s.at[r], cs_r.at[r], "noise", nz, mz)

    def combine(st, r, size, m):
        tops = [st[r, k, 0:m, :] for k in range(size)]
        top = functools.reduce(jnp.maximum, tops)
        mass = sum(st[r, k, m:2 * m, :] * jnp.exp(tops[k] - top) for k in range(size))
        return top + jnp.log(mass)

    def log_mass(st, size, m):
        count = sum(st[0, k, 2 * m:2 * m + 1, :] for k in range(size))
        return -jnp.log(count * float(BLOCK))

    def set_row(ref, v):
        for c in range(nr):
            ref[:, c * BLOCK:(c + 1) * BLOCK] = v[c:c + 1, :]

    log_a = log_b = f = g = None
    for turn in range(ITERS):
        pending += row_pass(turn, False)
        if turn == 0:
            full = dfull[...].T
            hi, lo = split(full)
            yt[0] = hi.astype(F32)
            yt[1] = lo.astype(F32)
        arrive(rst.at[turn], rs_s.at[turn], rs_r.at[turn], "dp", n, me)
        if turn == 0:
            log_b = log_mass(rst, n, nr)
        f = -(combine(rst, turn, n, nr) + log_b)
        set_row(fmrow, jnp.where(live_i, f, -jnp.inf))
        pending += col_pass(turn)
        arrive(cst.at[turn], cs_s.at[turn], cs_r.at[turn], "noise", nz, mz)
        if turn == 0:
            log_a = log_mass(cst, nz, nc)
        g = -(combine(cst, turn, nz, nc) + log_a)
        set_gm(g)
    f_ref[...] = jnp.where(live_i, SMOOTHING_TEMP * f, 0.0)
    g_ref[...] = jnp.where(live_j, SMOOTHING_TEMP * g, 0.0)

    pending += row_pass(ITERS, True)

    set_row(fmrow, jnp.where(live_i, f + log_a, -jnp.inf))

    def plan(c, _):
        at = pl.ds(pl.multiple_of(c * BLOCK, BLOCK), BLOCK)
        hi, lo = split(jnp.exp(kt[:, at] + fmrow[:, at] + gmb[...]))
        dhi[:, at] = hi
        dlo[:, at] = lo
        return 0

    lax.fori_loop(0, nr, plan, 0)

    def project(t, _):
        at = pl.ds(pl.multiple_of(t * TILE, TILE), TILE)
        ptmp[:, at] = dot3(dhi[...], dlo[...], xhi[:, at], xlo[:, at])
        return 0

    lax.fori_loop(0, coords // TILE, project, 0)
    for k in range(nz):
        pbuf[k] = ptmp[:, k * cz:(k + 1) * cz]
    for o in range(1, nz):
        to = lax.rem(mz + o, nz)
        c = copy(pbuf.at[to], zbuf.at[o], z_s.at[o], z_r.at[o], "noise", to)
        c.start()
        pending.append(c)

    arrive(rst.at[ITERS], rs_s.at[ITERS], rs_r.at[ITERS], "dp", n, me)
    level = combine(rst, ITERS, n, nr)
    set_row(facrow, jnp.where(live_i, jnp.exp(rst[ITERS, me, 0:nr, :] - level), 0.0))

    core = lax.rem(me, 2)

    def flip(w):
        return w * (1 - 2 * lax.rem(me // w, 2))

    delta = [flip(1)] + [(1 - core) * flip(1 << s) + core * flip(1 << (steps - s)) for s in range(1, steps)]

    def owner(q):
        d = me
        for s in range(steps):
            if (q >> s) & 1:
                d = d + delta[s]
        return d

    def landed(s, q):
        if s > 0:
            return q - (1 << s)
        return sum(1 << (steps - t) for t in range(1, steps) if (q >> t) & 1)

    slot = {}
    for s in range(steps):
        for q in range(0, n, 2 << s):
            slot[s, q] = len(slot)

    def half(odd):
        qs = list(range(odd, n, 2))
        hi = jnp.concatenate([yt[0, pl.ds(pl.multiple_of(owner(q) * cb, cb), cb), :] for q in qs], axis=0).astype(BF16)
        lo = jnp.concatenate([yt[1, pl.ds(pl.multiple_of(owner(q) * cb, cb), cb), :] for q in qs], axis=0).astype(BF16)

        def body(t, _):
            at = pl.ds(pl.multiple_of(t * TILE, TILE), TILE)
            out = dot3(hi, lo, whi[:, at], wlo[:, at]) * facrow[:, at]
            for m, q in enumerate(qs):
                acc[q, :, at] = out[m * cb:(m + 1) * cb, :]
            return 0

        lax.fori_loop(0, rows // TILE, body, 0)

    def hop(s, q):
        to = landed(s, q)
        return copy(acc.at[q], rb.at[slot[s, to]], h_s.at[q], h_r.at[slot[s, to]], "dp", me + delta[s])

    def take(s, q):
        copy(acc.at[q], rb.at[slot[s, q]], h_s.at[q], h_r.at[slot[s, q]], "dp", me + delta[s]).wait_recv()
        acc[q] += rb[slot[s, q]]

    half(1)
    for q in range(1, n, 2):
        c = hop(0, q)
        c.start()
        pending.append(c)
    half(0)
    for s in range(1, steps):
        for q in range(1 << s, n, 2 << s):
            take(s - 1, q)
            c = hop(s, q)
            c.start()
            pending.append(c)
        for q in range(0, n, 2 << s):
            take(s - 1, q)

    total = pbuf[mz]
    for o in range(1, nz):
        copy(pbuf.at[mz], zbuf.at[o], z_s.at[o], z_r.at[o], "noise", lax.rem(mz + o, nz)).wait_recv()
        total = total + zbuf[o]
    dt_ref[...] = total.T

    take(steps - 1, 0)
    nt_ref[...] = acc[0]
    for c in pending:
        c.wait_send()


def on_device(n, nz, x, y, nb, db):
    rows, coords = x.shape
    cols, cz = y.shape
    nr, nc = rows // BLOCK, cols // BLOCK
    cb = coords // n
    steps = n.bit_length() - 1
    crow = -(-(2 * nc + 1) // 8) * 8
    vm = pltpu.VMEM
    dma = lambda *s: pltpu.SemaphoreType.DMA(s)
    macs = rows * cols * coords
    f, g, nt, dt = pl.pallas_call(
        functools.partial(kernel, n, nz),
        out_shape=(
            jax.ShapeDtypeStruct((nr, BLOCK), F32),
            jax.ShapeDtypeStruct((nc, BLOCK), F32),
            jax.ShapeDtypeStruct((cb, rows), F32),
            jax.ShapeDtypeStruct((cz, cols), F32),
        ),
        in_specs=[pl.BlockSpec(memory_space=vm)] * 2 + [pl.BlockSpec(memory_space=pltpu.SMEM)] * 2,
        out_specs=(pl.BlockSpec(memory_space=vm),) * 4,
        scratch_shapes=[
            vm((nz, cols, cz), F32), vm((cols, coords), F32), vm((2, coords, cols), F32),
            vm((cols, rows), F32), vm((cols, BLOCK), F32), vm((1, rows), F32), vm((1, rows), F32),
            vm((1, rows), F32), vm((rows, coords), BF16), vm((rows, coords), BF16),
            vm((cols, rows), BF16), vm((cols, rows), BF16), vm((cols, rows), BF16), vm((cols, rows), BF16),
            vm((ITERS + 1, n, 2 * nr + 8, BLOCK), F32), vm((ITERS, nz, crow, BLOCK), F32),
            vm((n, cb, rows), F32), vm((n - 1, cb, rows), F32),
            vm((cols, coords), F32), vm((nz, cols, cz), F32), vm((nz, cols, cz), F32),
            dma(nz), dma(nz), dma(ITERS + 1, n), dma(ITERS + 1, n), dma(ITERS, nz), dma(ITERS, nz),
            dma(n), dma(n), dma(nz), dma(nz),
        ],
        compiler_params=pltpu.CompilerParams(
            collective_id=0, has_side_effects=True, vmem_limit_bytes=48 << 20),
        cost_estimate=pl.CostEstimate(flops=24 * macs, bytes_accessed=16 << 20, transcendentals=9 * rows * cols),
    )(x, y, nb, db)
    return f.reshape(rows), g.reshape(cols), nt, dt


def solution(mesh):
    return jax.shard_map(
        functools.partial(on_device, mesh.shape["dp"], mesh.shape["noise"]),
        mesh=mesh,
        in_specs=(P("noise", None), P("dp", "noise"), P("noise"), P("dp")),
        out_specs=(P("noise"), P("dp"), P("dp", "noise"), P("noise", "dp")),
        check_vma=False,
    )
```

time: 284 us -> 93.7 us (0.33)
  blocking collectives: 186 us -> 0 us
  Pallas kernels: 0 us -> 86.1 us
  waiting for transfers between devices: 42.2 us -> 0 us
  matrix products: 19.1 us -> 0 us
  between operations: 17.1 us -> 1.94 us
  other arithmetic: 10.7 us -> 0 us
    all_gather x15 -> x0, blocking collectives: 160 us -> none  [the longest x14 141 us: combined_all(): everything = jax.tree.map(lambda part: lax.all_gather(part, axis), shard)]
    pallas_call x0 -> x1, Pallas kernels: none -> 86.1 us  [on_device(): pl.pallas_call(functools.partial(kernel, n, nz), out_shape=(jax.ShapeDtyp...]
    unnamed x3 -> x0, waiting for transfers between devices: 42.2 us -> none
    psum x2 -> x0, blocking collectives: 26.4 us -> none  [the longest x1 15.6 us: on_device(): data_total = lax.psum((data_blocks * BLOCK).astype(jnp.float32), 'dp')]
    dot_general x3 -> x0, matrix products: 19.1 us -> none  [the longest x1 7.45 us: on_device(): lax.dot_general(coords, noise_weights, (((0,), (1,)), ((), ())), precisio...]
    reduce_sum x9 -> x0, other arithmetic: 7.21 us -> none  [the longest x4 2.76 us: row_threshold(): mass = jnp.sum(jnp.exp(pair_scores - local[:, None]), axis=1)]
  transfers between devices with their start and end apart: 2 -> 0, of which waited for: 1 -> 0; matrix products, arithmetic and copies ran while one was open for 5% -> 0% of each run, Pallas kernels for 0% -> 0%
where the time goes in v1:
time: 93.7 us; the launch traced here: 93.5 us
  Pallas kernels  86.1 us (92%)
  local copies, waits for them, and re-layouts  5.41 us (6%)
  between operations  1.94 us (2%)
    pallas_call x1, Pallas kernels, on_device(): pl.pallas_call(functools.partial(kernel, n, nz), out_shape=(jax.ShapeDtyp...  86.1 us
    unnamed x8, local copies, waits for them, and re-layouts  5.41 us

profile of v1, /device:TPU:0, one launch (start us, length us, event | category | flops | bytes accessed | tf_op | source)
XLA Modules:
  0.0 93.5 jit_solution(5524954500667459852)
XLA Ops:
  1.9 0.0 copy-start
  1.9 1.9 %copy-done = f32[1536,512]{1,0:T(8,128)S(1)} copy-done((f32[1536,512]{1,0:T(8,128)S(1)}, f32[1536,512]{1,0:T(8,128)}, u32[]{:S(2)}) %copy-start) | copy-done | bytes 3145752
  3.8 0.0 copy-start.1
  3.8 0.9 copy-done.1
  4.7 86.1 %shard_map.75 = (f32[12,128]{1,0:T(8,128)S(1)}, f32[3,128]{1,0:T(4,128)S(1)}, f32[64,1536]{1,0:T(8,128)S(1)}, f32[128,384]{1,0:T(8,128)S(1)}) custom-call(f32[1536,512]{1,0:T(8,128)S(1)} %copy-done, f32[384,128]{1,0:T(8,128)S(1)} %copy-done.1, s32[1]{0:T(128)S(6)} %copy.12.nb_ref, s32[1]{0:T(128)S(6)} %copy.13.db_ref), custom_call_target="tpu_custom_call" | custom-call | flops 7247757312 | bytes 16777216 | tf_op jit(solution)/shard_map/pallas_call | solution.py:292
  90.9 0.6 copy.14
  91.5 0.6 copy.15
  92.0 0.7 copy.16
  92.8 0.7 copy.17
Async XLA Ops:
  1.9 1.9 %copy-start = (f32[1536,512]{1,0:T(8,128)S(1)}, f32[1536,512]{1,0:T(8,128)}, u32[]{:S(2)}) copy-start(f32[1536,512]{1,0:T(8,128)} %x_ref.1) | copy-start | bytes 9437188
  3.8 0.9 copy-start.1

commit v2 on v1

--- a/solution.py
+++ b/solution.py
@@ -28,9 +28,9 @@
 
 
 def kernel(n, nz, x_ref, y_ref, nb_ref, db_ref, f_ref, g_ref, nt_ref, dt_ref,
-           dbuf, dfull, yt, kt, gmb, fmrow, facrow, xsq, xhi, xlo, whi, wlo, dhi, dlo,
+           xs, xv, dbuf, yt, kt, gmb, fmrow, facrow, loc, xsq, xhi, xlo, whi, wlo, dhi, dlo,
            rst, cst, acc, rb, ptmp, pbuf, zbuf,
-           ag_s, ag_r, rs_s, rs_r, cs_s, cs_r, h_s, h_r, z_s, z_r):
+           in_s, ag_s, ag_r, rs_s, rs_r, cs_s, cs_r, h_s, h_r, zs_s, z_r):
     me = lax.axis_index("dp")
     mz = lax.axis_index("noise")
     rows, coords = x_ref.shape
@@ -39,6 +39,11 @@
     cb = coords // n
     steps = n.bit_length() - 1
 
+    xin = pltpu.make_async_copy(x_ref, xv, in_s.at[0])
+    yin = pltpu.make_async_copy(y_ref, dbuf.at[mz], in_s.at[1])
+    yin.start()
+    xin.start()
+
     barrier = pltpu.get_barrier_semaphore()
     for o in range(1, n):
         pl.semaphore_signal(barrier, inc=1, device_id={"dp": lax.rem(me + o, n)}, device_id_type=MESH)
@@ -65,14 +70,30 @@
             copy(buf.at[src], buf.at[src], ssem.at[o], rsem.at[src], axis, src).wait_recv()
 
     pending = []
-    dbuf[mz] = y_ref[...]
-    pending += spread(dbuf, ag_s, ag_r, "noise", nz, mz)
+    def ag(way, src, o):
+        to = mz + 1 if way == 0 else mz - 1
+        return copy(dbuf.at[src], dbuf.at[src], ag_s.at[way, o], ag_r.at[src], "noise", to)
+
+    def has(way, o):
+        return mz >= o if way == 0 else mz + o < nz
+
+    def onward(way):
+        return mz + 1 < nz if way == 0 else mz >= 1
+
+    yin.wait()
+    for way in range(2):
+        @pl.when(onward(way))
+        def _():
+            ag(way, mz, 0).start()
+    xin.wait()
 
     ones = jnp.ones((8, coords), F32)
 
     def prep(t, _):
         at = pl.ds(pl.multiple_of(t * TILE, TILE), TILE)
-        x = x_ref[at, :]
+        x = xv[at, :]
+        for k in range(nz):
+            xs[k, at, :] = x[:, k * cz:(k + 1) * cz]
         hi, lo = split(x)
         xhi[at, :] = hi
         xlo[at, :] = lo
@@ -94,19 +115,41 @@
 
     set_gm(jnp.zeros((nc, BLOCK), F32))
 
-    arrive(dbuf, ag_s, ag_r, "noise", nz, mz)
-    for k in range(nz):
-        dfull[:, k * cz:(k + 1) * cz] = dbuf[k]
-    ysq = jnp.sum(dfull[...] * dfull[...], axis=1, keepdims=True)
-
-    def cost(t, _):
-        at = pl.ds(pl.multiple_of(t * TILE, TILE), TILE)
-        cross = lax.dot_general(dfull[...], x_ref[at, :], NT, precision=lax.Precision.HIGHEST,
-                                preferred_element_type=F32)
-        kt[:, at] = (2.0 * cross - (xsq[:, at] + ysq)) * (1.0 / SMOOTHING_TEMP)
-        return 0
-
-    lax.fori_loop(0, rows // TILE, cost, 0)
+    def cost(src, first):
+        y = dbuf[src]
+        ysq = jnp.sum(y * y, axis=1, keepdims=True)
+
+        def body(t, _):
+            at = pl.ds(pl.multiple_of(t * TILE, TILE), TILE)
+            cross = lax.dot_general(y, xs[src, at, :], NT, precision=lax.Precision.HIGHEST,
+                                    preferred_element_type=F32)
+            if first:
+                kt[:, at] = (2.0 * cross - (xsq[:, at] + ysq)) * (1.0 / SMOOTHING_TEMP)
+            else:
+                kt[:, at] += (2.0 * cross - ysq) * (1.0 / SMOOTHING_TEMP)
+            return 0
+
+        lax.fori_loop(0, rows // TILE, body, 0)
+
+    cost(mz, True)
+    for o in range(1, nz):
+        for way in range(2):
+            src = mz - o if way == 0 else mz + o
+
+            @pl.when(has(way, o))
+            def _():
+                ag(way, src, o).wait_recv()
+
+                @pl.when(onward(way))
+                def _():
+                    ag(way, src, o).start()
+
+        for way in range(2):
+            src = mz - o if way == 0 else mz + o
+
+            @pl.when(has(way, o))
+            def _():
+                cost(src, False)
 
     def row_pass(r, keep):
         def body(c, _):
@@ -114,16 +157,16 @@
             s = kt[:, at] + gmb[...]
             top = jnp.max(s, axis=0, keepdims=True)
             e = jnp.exp(s - top)
-            rst[r, me, pl.ds(c, 1), :] = top
-            rst[r, me, pl.ds(nr + c, 1), :] = jnp.sum(e, axis=0, keepdims=True)
+            rst[r, me, pl.ds(c, 1), :] = top + jnp.log(jnp.sum(e, axis=0, keepdims=True))
             if keep:
+                loc[pl.ds(c, 1), :] = top
                 hi, lo = split(e)
                 whi[:, at] = hi
                 wlo[:, at] = lo
             return 0
 
         lax.fori_loop(0, nr, body, 0)
-        rst[r, me, 2 * nr:2 * nr + 8, :] = jnp.full((8, BLOCK), db_ref[0].astype(F32), F32)
+        rst[r, me, nr:nr + 1, :] = jnp.full((1, BLOCK), db_ref[0].astype(F32), F32)
         return spread(rst.at[r], rs_s.at[r], rs_r.at[r], "dp", n, me)
 
     def col_pass(r):
@@ -131,22 +174,21 @@
             s = kt[pl.ds(pl.multiple_of(k * BLOCK, BLOCK), BLOCK), :] + fmrow[...]
             top = jnp.max(s, axis=1, keepdims=True)
             mass = jnp.sum(jnp.exp(s - top), axis=1, keepdims=True)
-            cst[r, mz, pl.ds(k, 1), :] = jnp.sum(jnp.where(eye, top, 0.0), axis=0, keepdims=True)
-            cst[r, mz, pl.ds(nc + k, 1), :] = jnp.sum(jnp.where(eye, mass, 0.0), axis=0, keepdims=True)
+            cst[r, mz, pl.ds(k, 1), :] = jnp.sum(jnp.where(eye, top + jnp.log(mass), 0.0), axis=0, keepdims=True)
             return 0
 
         lax.fori_loop(0, nc, body, 0)
-        cst[r, mz, 2 * nc:2 * nc + 1, :] = jnp.full((1, BLOCK), nb_ref[0].astype(F32), F32)
+        cst[r, mz, nc:nc + 1, :] = jnp.full((1, BLOCK), nb_ref[0].astype(F32), F32)
         return spread(cst.at[r], cs_s.at[r], cs_r.at[r], "noise", nz, mz)
 
     def combine(st, r, size, m):
         tops = [st[r, k, 0:m, :] for k in range(size)]
         top = functools.reduce(jnp.maximum, tops)
-        mass = sum(st[r, k, m:2 * m, :] * jnp.exp(tops[k] - top) for k in range(size))
+        mass = sum(jnp.exp(t - top) for t in tops)
         return top + jnp.log(mass)
 
     def log_mass(st, size, m):
-        count = sum(st[0, k, 2 * m:2 * m + 1, :] for k in range(size))
+        count = sum(st[0, k, m:m + 1, :] for k in range(size))
         return -jnp.log(count * float(BLOCK))
 
     def set_row(ref, v):
@@ -157,7 +199,7 @@
     for turn in range(ITERS):
         pending += row_pass(turn, False)
         if turn == 0:
-            full = dfull[...].T
+            full = jnp.concatenate([dbuf[k] for k in range(nz)], axis=1).T
             hi, lo = split(full)
             yt[0] = hi.astype(F32)
             yt[1] = lo.astype(F32)
@@ -196,15 +238,36 @@
     lax.fori_loop(0, coords // TILE, project, 0)
     for k in range(nz):
         pbuf[k] = ptmp[:, k * cz:(k + 1) * cz]
-    for o in range(1, nz):
-        to = lax.rem(mz + o, nz)
-        c = copy(pbuf.at[to], zbuf.at[o], z_s.at[o], z_r.at[o], "noise", to)
-        c.start()
-        pending.append(c)
+
+    def zsend(way, to):
+        side = mz + 1 if way == 0 else mz - 1
+        return copy(pbuf.at[to], zbuf.at[way, to], zs_s.at[way, to], z_r.at[way, to], "noise", side)
+
+    rank = (mz, nz - 1 - mz)
+
+    def target(way, t):
+        return t if way == 0 else nz - 1 - t
+
+    for way in range(2):
+        @pl.when(rank[way] == 0)
+        def _():
+            for t in range(nz - 1, 0, -1):
+                zsend(way, target(way, t)).start()
+
+    def relay(turn):
+        for way in range(2):
+            t = nz - 1 - turn + rank[way]
+
+            @pl.when((rank[way] >= 1) & (rank[way] <= turn))
+            def _():
+                to = target(way, t)
+                zsend(way, to).wait_recv()
+                pbuf[to] += zbuf[way, to]
+                zsend(way, to).start()
 
     arrive(rst.at[ITERS], rs_s.at[ITERS], rs_r.at[ITERS], "dp", n, me)
     level = combine(rst, ITERS, n, nr)
-    set_row(facrow, jnp.where(live_i, jnp.exp(rst[ITERS, me, 0:nr, :] - level), 0.0))
+    set_row(facrow, jnp.where(live_i, jnp.exp(loc[...] - level), 0.0))
 
     core = lax.rem(me, 2)
 
@@ -230,51 +293,86 @@
         for q in range(0, n, 2 << s):
             slot[s, q] = len(slot)
 
-    def half(odd):
+    parts = 2 if rows % (2 * TILE) == 0 else 1
+    wide = rows // parts
+
+    def lows(q):
+        return (q & -q) if q else n
+
+    def half(odd, h):
         qs = list(range(odd, n, 2))
         hi = jnp.concatenate([yt[0, pl.ds(pl.multiple_of(owner(q) * cb, cb), cb), :] for q in qs], axis=0).astype(BF16)
         lo = jnp.concatenate([yt[1, pl.ds(pl.multiple_of(owner(q) * cb, cb), cb), :] for q in qs], axis=0).astype(BF16)
 
         def body(t, _):
-            at = pl.ds(pl.multiple_of(t * TILE, TILE), TILE)
+            at = pl.ds(pl.multiple_of(h * wide + t * TILE, TILE), TILE)
             out = dot3(hi, lo, whi[:, at], wlo[:, at]) * facrow[:, at]
             for m, q in enumerate(qs):
                 acc[q, :, at] = out[m * cb:(m + 1) * cb, :]
             return 0
 
-        lax.fori_loop(0, rows // TILE, body, 0)
-
-    def hop(s, q):
-        to = landed(s, q)
-        return copy(acc.at[q], rb.at[slot[s, to]], h_s.at[q], h_r.at[slot[s, to]], "dp", me + delta[s])
-
-    def take(s, q):
-        copy(acc.at[q], rb.at[slot[s, q]], h_s.at[q], h_r.at[slot[s, q]], "dp", me + delta[s]).wait_recv()
-        acc[q] += rb[slot[s, q]]
-
-    half(1)
-    for q in range(1, n, 2):
-        c = hop(0, q)
+        lax.fori_loop(0, wide // TILE, body, 0)
+
+    def link(s, q, to, h):
+        at = pl.ds(h * wide, wide)
+        i = slot[s, to]
+        return copy(acc.at[q, :, at], rb.at[i, :, at], h_s.at[q, h], h_r.at[i, h], "dp", me + delta[s])
+
+    def hop(s, q, h):
+        c = link(s, q, landed(s, q), h)
         c.start()
         pending.append(c)
-    half(0)
+
+    def take(s, q, h):
+        link(s, q, q, h).wait_recv()
+        at = pl.ds(h * wide, wide)
+        acc[q, :, at] += rb[slot[s, q], :, at]
+
+    def urgent(q):
+        return (lows(q), -q)
+
+    for h in range(parts):
+        half(1, h)
+        for q in sorted(range(1, n, 2), key=lambda q: urgent(landed(0, q))):
+            hop(0, q, h)
+    for h in range(parts):
+        half(0, h)
+    turn = 1
     for s in range(1, steps):
-        for q in range(1 << s, n, 2 << s):
-            take(s - 1, q)
-            c = hop(s, q)
-            c.start()
-            pending.append(c)
-        for q in range(0, n, 2 << s):
-            take(s - 1, q)
-
-    total = pbuf[mz]
-    for o in range(1, nz):
-        copy(pbuf.at[mz], zbuf.at[o], z_s.at[o], z_r.at[o], "noise", lax.rem(mz + o, nz)).wait_recv()
-        total = total + zbuf[o]
-    dt_ref[...] = total.T
-
-    take(steps - 1, 0)
+        for q in sorted(range(1 << s, n, 2 << s), key=lambda q: urgent(landed(s, q))):
+            for h in range(parts):
+                take(s - 1, q, h)
+                hop(s, q, h)
+        for q in sorted(range(0, n, 2 << s), key=urgent):
+            if q == 0 or s == steps - 1:
+                if turn < nz - 1:
+                    relay(turn)
+                    turn += 1
+            for h in range(parts):
+                take(s - 1, q, h)
+    for late in range(turn, nz - 1):
+        relay(late)
+
+    dt_ref[...] = pbuf[mz].T
+    for way in range(2):
+        @pl.when(rank[way] >= 1)
+        def _():
+            zsend(way, mz).wait_recv()
+            dt_ref[...] += zbuf[way, mz].T
+
+    for h in range(parts):
+        take(steps - 1, 0, h)
     nt_ref[...] = acc[0]
+    for way in range(2):
+        for o in range(nz - 1):
+            @pl.when(has(way, o) & onward(way))
+            def _():
+                ag(way, mz - o if way == 0 else mz + o, o).wait_send()
+
+        for t in range(1, nz):
+            @pl.when(rank[way] < t)
+            def _():
+                zsend(way, target(way, t)).wait_send()
     for c in pending:
         c.wait_send()
 
@@ -285,7 +383,7 @@
     nr, nc = rows // BLOCK, cols // BLOCK
     cb = coords // n
     steps = n.bit_length() - 1
-    crow = -(-(2 * nc + 1) // 8) * 8
+    up = lambda k: -(-k // 8) * 8
     vm = pltpu.VMEM
     dma = lambda *s: pltpu.SemaphoreType.DMA(s)
     macs = rows * cols * coords
@@ -297,21 +395,21 @@
             jax.ShapeDtypeStruct((cb, rows), F32),
             jax.ShapeDtypeStruct((cz, cols), F32),
         ),
-        in_specs=[pl.BlockSpec(memory_space=vm)] * 2 + [pl.BlockSpec(memory_space=pltpu.SMEM)] * 2,
+        in_specs=[pl.BlockSpec(memory_space=pltpu.HBM)] * 2 + [pl.BlockSpec(memory_space=pltpu.SMEM)] * 2,
         out_specs=(pl.BlockSpec(memory_space=vm),) * 4,
         scratch_shapes=[
-            vm((nz, cols, cz), F32), vm((cols, coords), F32), vm((2, coords, cols), F32),
+            vm((nz, rows, cz), F32), vm((rows, coords), F32), vm((nz, cols, cz), F32), vm((2, coords, cols), F32),
             vm((cols, rows), F32), vm((cols, BLOCK), F32), vm((1, rows), F32), vm((1, rows), F32),
-            vm((1, rows), F32), vm((rows, coords), BF16), vm((rows, coords), BF16),
+            vm((nr, BLOCK), F32), vm((1, rows), F32), vm((rows, coords), BF16), vm((rows, coords), BF16),
             vm((cols, rows), BF16), vm((cols, rows), BF16), vm((cols, rows), BF16), vm((cols, rows), BF16),
-            vm((ITERS + 1, n, 2 * nr + 8, BLOCK), F32), vm((ITERS, nz, crow, BLOCK), F32),
+            vm((ITERS + 1, n, up(nr + 1), BLOCK), F32), vm((ITERS, nz, up(nc + 1), BLOCK), F32),
             vm((n, cb, rows), F32), vm((n - 1, cb, rows), F32),
-            vm((cols, coords), F32), vm((nz, cols, cz), F32), vm((nz, cols, cz), F32),
-            dma(nz), dma(nz), dma(ITERS + 1, n), dma(ITERS + 1, n), dma(ITERS, nz), dma(ITERS, nz),
-            dma(n), dma(n), dma(nz), dma(nz),
+            vm((cols, coords), F32), vm((nz, cols, cz), F32), vm((2, nz, cols, cz), F32),
+            dma(2), dma(2, nz), dma(nz), dma(ITERS + 1, n), dma(ITERS + 1, n), dma(ITERS, nz), dma(ITERS, nz),
+            dma(n, 2), dma(n, 2), dma(2, nz), dma(2, nz),
         ],
         compiler_params=pltpu.CompilerParams(
-            collective_id=0, has_side_effects=True, vmem_limit_bytes=48 << 20),
+            collective_id=0, has_side_effects=True, vmem_limit_bytes=56 << 20),
         cost_estimate=pl.CostEstimate(flops=24 * macs, bytes_accessed=16 << 20, transcendentals=9 * rows * cols),
     )(x, y, nb, db)
     return f.reshape(rows), g.reshape(cols), nt, dt

time: 93.7 us -> 90 us (0.961)
  Pallas kernels: 86.1 us -> 81.8 us
    pallas_call x1, Pallas kernels: 86.1 us -> 81.8 us  [on_device(): pl.pallas_call(functools.partial(kernel, n, nz), out_shape=(jax.ShapeDtyp...]
    unnamed x8 -> x4, local copies, waits for them, and re-layouts: 5.41 us -> 5.93 us
where the time goes in v2:
time: 90 us; the launch traced here: 89.7 us
  Pallas kernels  81.8 us (91%)
  local copies, waits for them, and re-layouts  5.93 us (7%)
  between operations  1.93 us (2%)
    pallas_call x1, Pallas kernels, on_device(): pl.pallas_call(functools.partial(kernel, n, nz), out_shape=(jax.ShapeDtyp...  81.8 us
    unnamed x4, local copies, waits for them, and re-layouts  5.93 us

profile of v2, /device:TPU:0, one launch (start us, length us, event | category | flops | bytes accessed | tf_op | source)
XLA Modules:
  0.0 89.7 jit_solution(12307072925573438502)
XLA Ops:
  1.9 81.8 %shard_map.75 = (f32[12,128]{1,0:T(8,128)}, f32[3,128]{1,0:T(4,128)}, f32[64,1536]{1,0:T(8,128)}, f32[128,384]{1,0:T(8,128)}) custom-call(f32[1536,512]{1,0:T(8,128)} %x_ref.1, f32[384,128]{1,0:T(8,128)} %y_ref.1, s32[1]{0:T(128)S(6)} %copy.12.nb_ref, s32[1]{0:T(128)S(6)} %copy.13.db_ref), custom_call_target="tpu_custom_call" | custom-call | flops 7247757312 | bytes 16777216 | tf_op jit(solution)/shard_map/pallas_call | solution.py:390
  83.8 1.3 %copy.14 = f32[1536]{0:T(1024)} copy(f32[1536]{0:T(1024)} %bitcast.2) | data formatting | bytes 12288
  85.1 1.2 %copy.15 = f32[384]{0:T(512)} copy(f32[384]{0:T(512)} %bitcast.3) | data formatting | bytes 3072
  86.3 1.8 %copy.16 = f32[64,1536]{1,0:T(8,128)} copy(f32[64,1536]{1,0:T(8,128)} %get-tuple-element.18) | data formatting | bytes 786432
  88.1 1.6 %copy.17 = f32[128,384]{1,0:T(8,128)} copy(f32[128,384]{1,0:T(8,128)} %get-tuple-element.19) | data formatting | bytes 393216

commit v3 on v2

--- a/solution.py
+++ b/solution.py
@@ -70,9 +70,10 @@
             copy(buf.at[src], buf.at[src], ssem.at[o], rsem.at[src], axis, src).wait_recv()
 
     pending = []
-    def ag(way, src, o):
+    def ag(way, src, o, p):
         to = mz + 1 if way == 0 else mz - 1
-        return copy(dbuf.at[src], dbuf.at[src], ag_s.at[way, o], ag_r.at[src], "noise", to)
+        piece = dbuf.at[src, p * BLOCK:(p + 1) * BLOCK, :]
+        return copy(piece, piece, ag_s.at[way, o, p], ag_r.at[src, p], "noise", to)
 
     def has(way, o):
         return mz >= o if way == 0 else mz + o < nz
@@ -84,7 +85,8 @@
     for way in range(2):
         @pl.when(onward(way))
         def _():
-            ag(way, mz, 0).start()
+            for p in range(nc):
+                ag(way, mz, 0, p).start()
     xin.wait()
 
     ones = jnp.ones((8, coords), F32)
@@ -133,16 +135,16 @@
 
     cost(mz, True)
     for o in range(1, nz):
-        for way in range(2):
+        for p, way in [(p, way) for p in range(nc) for way in range(2)]:
             src = mz - o if way == 0 else mz + o
 
             @pl.when(has(way, o))
             def _():
-                ag(way, src, o).wait_recv()
+                ag(way, src, o, p).wait_recv()
 
                 @pl.when(onward(way))
                 def _():
-                    ag(way, src, o).start()
+                    ag(way, src, o, p).start()
 
         for way in range(2):
             src = mz - o if way == 0 else mz + o
@@ -344,12 +346,11 @@
                 take(s - 1, q, h)
                 hop(s, q, h)
         for q in sorted(range(0, n, 2 << s), key=urgent):
-            if q == 0 or s == steps - 1:
-                if turn < nz - 1:
-                    relay(turn)
-                    turn += 1
             for h in range(parts):
                 take(s - 1, q, h)
+        if turn < nz - 1:
+            relay(turn)
+            turn += 1
     for late in range(turn, nz - 1):
         relay(late)
 
@@ -367,7 +368,8 @@
         for o in range(nz - 1):
             @pl.when(has(way, o) & onward(way))
             def _():
-                ag(way, mz - o if way == 0 else mz + o, o).wait_send()
+                for p in range(nc):
+                    ag(way, mz - o if way == 0 else mz + o, o, p).wait_send()
 
         for t in range(1, nz):
             @pl.when(rank[way] < t)
@@ -405,11 +407,11 @@
             vm((ITERS + 1, n, up(nr + 1), BLOCK), F32), vm((ITERS, nz, up(nc + 1), BLOCK), F32),
             vm((n, cb, rows), F32), vm((n - 1, cb, rows), F32),
             vm((cols, coords), F32), vm((nz, cols, cz), F32), vm((2, nz, cols, cz), F32),
-            dma(2), dma(2, nz), dma(nz), dma(ITERS + 1, n), dma(ITERS + 1, n), dma(ITERS, nz), dma(ITERS, nz),
+            dma(2), dma(2, nz, nc), dma(nz, nc), dma(ITERS + 1, n), dma(ITERS + 1, n), dma(ITERS, nz), dma(ITERS, nz),
             dma(n, 2), dma(n, 2), dma(2, nz), dma(2, nz),
         ],
         compiler_params=pltpu.CompilerParams(
-            collective_id=0, has_side_effects=True, vmem_limit_bytes=56 << 20),
+            collective_id=0, has_side_effects=True, vmem_limit_bytes=44 << 20),
         cost_estimate=pl.CostEstimate(flops=24 * macs, bytes_accessed=16 << 20, transcendentals=9 * rows * cols),
     )(x, y, nb, db)
     return f.reshape(rows), g.reshape(cols), nt, dt

time: 90 us -> 93.1 us (1.034)
  Pallas kernels: 81.8 us -> 85.6 us
    pallas_call x1, Pallas kernels: 81.8 us -> 85.6 us  [on_device(): pl.pallas_call(functools.partial(kernel, n, nz), out_shape=(jax.ShapeDtyp...]
    unnamed x4 -> x8, local copies, waits for them, and re-layouts: 5.93 us -> 5.41 us
where the time goes in v3:
time: 93.1 us; the launch traced here: 92.9 us
  Pallas kernels  85.6 us (92%)
  local copies, waits for them, and re-layouts  5.41 us (6%)
  between operations  1.94 us (2%)
    pallas_call x1, Pallas kernels, on_device(): pl.pallas_call(functools.partial(kernel, n, nz), out_shape=(jax.ShapeDtyp...  85.6 us
    unnamed x8, local copies, waits for them, and re-layouts  5.41 us

profile of v3, /device:TPU:0, one launch (start us, length us, event | category | flops | bytes accessed | tf_op | source)
XLA Modules:
  0.0 92.9 jit_solution(1561239699281897593)
XLA Ops:
  1.9 0.0 copy-start
  1.9 1.9 %copy-done = f32[1536,512]{1,0:T(8,128)S(1)} copy-done((f32[1536,512]{1,0:T(8,128)S(1)}, f32[1536,512]{1,0:T(8,128)}, u32[]{:S(2)}) %copy-start) | copy-done | bytes 3145752
  3.8 0.0 copy-start.1
  3.8 0.9 copy-done.1
  4.7 85.6 %shard_map.75 = (f32[12,128]{1,0:T(8,128)S(1)}, f32[3,128]{1,0:T(4,128)S(1)}, f32[64,1536]{1,0:T(8,128)S(1)}, f32[128,384]{1,0:T(8,128)S(1)}) custom-call(f32[1536,512]{1,0:T(8,128)S(1)} %copy-done, f32[384,128]{1,0:T(8,128)S(1)} %copy-done.1, s32[1]{0:T(128)S(6)} %copy.12.nb_ref, s32[1]{0:T(128)S(6)} %copy.13.db_ref), custom_call_target="tpu_custom_call" | custom-call | flops 7247757312 | bytes 16777216 | tf_op jit(solution)/shard_map/pallas_call | solution.py:392
  90.3 0.6 copy.14
  90.9 0.6 copy.15
  91.5 0.7 copy.16
  92.3 0.7 copy.17
Async XLA Ops:
  1.9 1.9 %copy-start = (f32[1536,512]{1,0:T(8,128)S(1)}, f32[1536,512]{1,0:T(8,128)}, u32[]{:S(2)}) copy-start(f32[1536,512]{1,0:T(8,128)} %x_ref.1) | copy-start | bytes 9437188
  3.8 0.9 copy-start.1

commit v4 on v3

--- a/solution.py
+++ b/solution.py
@@ -346,11 +346,12 @@
                 take(s - 1, q, h)
                 hop(s, q, h)
         for q in sorted(range(0, n, 2 << s), key=urgent):
+            if q == 0 or s == steps - 1:
+                if turn < nz - 1:
+                    relay(turn)
+                    turn += 1
             for h in range(parts):
                 take(s - 1, q, h)
-        if turn < nz - 1:
-            relay(turn)
-            turn += 1
     for late in range(turn, nz - 1):
         relay(late)
 
@@ -411,7 +412,7 @@
             dma(n, 2), dma(n, 2), dma(2, nz), dma(2, nz),
         ],
         compiler_params=pltpu.CompilerParams(
-            collective_id=0, has_side_effects=True, vmem_limit_bytes=44 << 20),
+            collective_id=0, has_side_effects=True, vmem_limit_bytes=56 << 20),
         cost_estimate=pl.CostEstimate(flops=24 * macs, bytes_accessed=16 << 20, transcendentals=9 * rows * cols),
     )(x, y, nb, db)
     return f.reshape(rows), g.reshape(cols), nt, dt

time: 93.1 us -> 90.2 us (0.969)
  Pallas kernels: 85.6 us -> 82.1 us
    pallas_call x1, Pallas kernels: 85.6 us -> 82.1 us  [on_device(): pl.pallas_call(functools.partial(kernel, n, nz), out_shape=(jax.ShapeDtyp...]
    unnamed x8 -> x4, local copies, waits for them, and re-layouts: 5.41 us -> 5.93 us
where the time goes in v4:
time: 90.2 us; the launch traced here: 89.9 us
  Pallas kernels  82.1 us (91%)
  local copies, waits for them, and re-layouts  5.93 us (7%)
  between operations  1.93 us (2%)
    pallas_call x1, Pallas kernels, on_device(): pl.pallas_call(functools.partial(kernel, n, nz), out_shape=(jax.ShapeDtyp...  82.1 us
    unnamed x4, local copies, waits for them, and re-layouts  5.93 us

profile of v4, /device:TPU:0, one launch (start us, length us, event | category | flops | bytes accessed | tf_op | source)
XLA Modules:
  0.0 89.9 jit_solution(5250011570354649400)
XLA Ops:
  1.9 82.1 %shard_map.75 = (f32[12,128]{1,0:T(8,128)}, f32[3,128]{1,0:T(4,128)}, f32[64,1536]{1,0:T(8,128)}, f32[128,384]{1,0:T(8,128)}) custom-call(f32[1536,512]{1,0:T(8,128)} %x_ref.1, f32[384,128]{1,0:T(8,128)} %y_ref.1, s32[1]{0:T(128)S(6)} %copy.12.nb_ref, s32[1]{0:T(128)S(6)} %copy.13.db_ref), custom_call_target="tpu_custom_call" | custom-call | flops 7247757312 | bytes 16777216 | tf_op jit(solution)/shard_map/pallas_call | solution.py:393
  84.0 1.3 %copy.14 = f32[1536]{0:T(1024)} copy(f32[1536]{0:T(1024)} %bitcast.2) | data formatting | bytes 12288
  85.3 1.2 %copy.15 = f32[384]{0:T(512)} copy(f32[384]{0:T(512)} %bitcast.3) | data formatting | bytes 3072
  86.5 1.8 %copy.16 = f32[64,1536]{1,0:T(8,128)} copy(f32[64,1536]{1,0:T(8,128)} %get-tuple-element.18) | data formatting | bytes 786432
  88.3 1.6 %copy.17 = f32[128,384]{1,0:T(8,128)} copy(f32[128,384]{1,0:T(8,128)} %get-tuple-element.19) | data formatting | bytes 393216
